TPU v7x, 32 devices: a whole 2x2x4 slice. The times are simulated.
32 devices in a mesh: blk: 8 (over z, y), gy: 4 (over x, core).
Axes of the slice: x: 2, y: 2, z: 4, core: 2. Of those that a mesh axis runs over, the one named last changes fastest.
Arguments:
- image: float32 [1, 2048, 2048], P(None, 'blk', 'gy'), may hold values from -6 to 6
- measured: float32 [1, 16, 2816], P(None, 'blk'), may hold values from -6 to 6
- row_weight: float32 [16, 2816], P('blk'), may hold values from 0.25 to 2
- col_weight: float32 [2048, 2048], P('blk', 'gy'), may hold values from 1 to 8
- band_weight: bfloat16 [16, 2048, 128], P('blk', 'gy'), may hold values from -0.01171875 to 0.01171875
- band_shift: int32 [16, 8], replicated, may hold values from 0 to 3
Outputs:
- updated: float32 [1, 2048, 2048], P(None, 'blk', 'gy')
Inputs may be any that keep to these rules, and one draw needn't show every extreme that they name: band_shift[t, s] is the number of panels by which slab s's footprint under tilt t starts beyond panel s * 2.
All inputs are finite; a program needn't handle non-finite values.
Results may differ from a plain program's by a relative error of at most 0.0025.
Values may be sent and summed in bfloat16 or wider, within the bound.
A program may use at most 64 MiB of HBM per device.

v0:
```python
import math
import jax
import jax.numpy as jnp
from jax import lax
from jax.sharding import PartitionSpec as P

PW = 128
SMOOTH = 0.25


def with_halo(cells, sides, width):
    for axis, dim in sides:
        count = lax.axis_size(axis)
        ends = count - 1
        head = lax.slice_in_dim(cells, 0, width, axis=dim)
        tail = lax.slice_in_dim(cells, cells.shape[dim] - width, cells.shape[dim], axis=dim)
        cells = jnp.concatenate(
            [
                lax.ppermute(tail, axis, [(i, (i + 1) % count) for i in range(ends)]),
                cells,
                lax.ppermute(head, axis, [((i + 1) % count, i) for i in range(ends)]),
            ],
            axis=dim,
        )
    return cells


def shift_rows(rows, direction):
    col_count = rows.shape[-2]
    bit_count = (col_count - 1).bit_length()
    column_index = jnp.arange(col_count, dtype=jnp.int32)[:, None]
    for level in range(bit_count):
        moved = jnp.roll(rows, direction * (1 << level), axis=-1)
        chosen = column_index >> level & 1 == 1
        rows = jnp.where(chosen, moved, rows)
    return rows


def diagonal_sum(product):
    leading = product.shape[:-2]
    col_count, band_width = product.shape[-2:]
    keep_pads = [(0, 0)] * (len(leading) + 1)
    padded = jnp.pad(product, keep_pads + [(0, col_count)])
    return jnp.sum(shift_rows(padded, 1), axis=-2)


def band_rows(panels, col_count, band_width):
    leading = panels.shape[:-1]
    window_len = panels.shape[-1]
    repeated = jnp.broadcast_to(panels[..., None, :], leading + (col_count, window_len))
    return shift_rows(repeated, -1)[..., :band_width]


def per_device(image, measured, row_weight, col_weight, band_weight, band_shift):
    row_count, col_count, depth_count = image.shape
    local_tilts = measured.shape[1]
    detector_len = measured.shape[2]
    band_width = band_weight.shape[2]
    window_len = col_count + band_width
    block_count = lax.axis_size("blk")
    myself = lax.axis_index("blk")
    tilt_count = local_tilts * block_count
    per_slab = col_count // PW
    zero_index = jnp.int32(0)
    copies = image.astype(jnp.bfloat16)
    slab_bins = ((jnp.arange(block_count, dtype=jnp.int32) * per_slab)[None, :] + band_shift) * PW
    first_tilt = myself * local_tilts
    own_bins = lax.dynamic_slice_in_dim(slab_bins, first_tilt, local_tilts, 0)
    group_size = math.gcd(tilt_count, 8)
    all_weights = lax.all_gather(band_weight, "blk", axis=0, tiled=True)
    weight_groups = all_weights.reshape(
        tilt_count // group_size, group_size, depth_count, band_width
    )

    def place_windows(running, windows, source):
        for tilt_slot in range(local_tilts):
            offset = own_bins[tilt_slot, source]
            corner = (zero_index, jnp.int32(tilt_slot), offset)
            current = lax.dynamic_slice(running, corner, (row_count, 1, window_len))
            running = lax.dynamic_update_slice(
                running, current + windows[tilt_slot][:, None, :], corner
            )
        return running

    initial = jnp.zeros((row_count, local_tilts, detector_len), jnp.float32)

    def project_group(weights):
        product = jnp.einsum("yiz,tzd->tyid", copies, weights, preferred_element_type=jnp.float32)
        return diagonal_sum(product)

    windows = lax.map(project_group, weight_groups)
    windows = windows.reshape(block_count, local_tilts, row_count, window_len)
    received = lax.all_to_all(windows, "blk", split_axis=0, concat_axis=0, tiled=True)

    def add_source(source, running):
        return place_windows(
            running, lax.dynamic_index_in_dim(received, source, 0, keepdims=False), source
        )

    partial_sum = lax.fori_loop(0, block_count, add_source, initial)
    projection = lax.psum(partial_sum, "gy")
    weighted = (row_weight[None] * (measured - projection)).astype(jnp.bfloat16)

    def cut_panels(slab_offsets):
        pieces = [
            lax.dynamic_slice(
                weighted[:, tilt_slot],
                (zero_index, slab_offsets[tilt_slot]),
                (row_count, window_len),
            )
            for tilt_slot in range(local_tilts)
        ]
        return jnp.stack(pieces, axis=1)

    outgoing = jax.vmap(cut_panels, in_axes=1, out_axes=1)(own_bins)
    arrived = lax.all_to_all(outgoing, "blk", split_axis=1, concat_axis=1, tiled=True)
    panels = arrived.reshape(row_count, tilt_count, window_len)
    panel_groups = panels.reshape(
        row_count, tilt_count // group_size, group_size, window_len
    ).transpose(1, 0, 2, 3)

    def back_group(running, operands):
        panel_part, weight_part = operands
        sheared = band_rows(panel_part, col_count, band_width)
        added = jnp.einsum(
            "ytid,tzd->yiz", sheared, weight_part, preferred_element_type=jnp.float32
        )
        return (running + added, None)

    start_back = jnp.zeros((row_count, col_count, depth_count), jnp.float32)
    backed, leftover = lax.scan(back_group, start_back, (panel_groups, weight_groups))
    padded_depth = with_halo(image.astype(jnp.bfloat16), (("gy", 2),), 1).astype(image.dtype)
    return (
        image
        + col_weight[None] * backed
        + SMOOTH * (padded_depth[:, :, :-2] + padded_depth[:, :, 2:] - 2.0 * image)
    )


def solution(mesh):
    return jax.shard_map(
        per_device,
        mesh=mesh,
        in_specs=(
            P(None, "blk", "gy"),
            P(None, "blk", None),
            P("blk", None),
            P("blk", "gy"),
            P("blk", "gy", None),
            P(),
        ),
        out_specs=P(None, "blk", "gy"),
        check_vma=False,
    )
```

profile of v0, /device:TPU:0, one launch (start us, length us, event | category | flops | bytes accessed | tf_op | source)
XLA Modules:
  0.0 203.8 jit_solution(14922307778124006677)
XLA Ops:
  7.3 1.1 convert_element_type.22
  9.0 3.0 %collective-permute-start = (bf16[1,256,1]{2,1,0:T(8,128)(2,1)}, bf16[1,256,1]{2,1,0:T(8,128)(2,1)}, u32[]{:S(2)}, u32[]{:S(2)}) collective-permute-start(bf16[1,256,1]{2,1,0:T(8,128)(2,1)} %get-tuple-element.283), channel_id=1, source_target_pairs={{0,1},{1,2},{2,3},{4,5},{5,6},{6,7},{8,9},{9,10},{10,11},{12,13},{... | collective-permute-start | bytes 1544 | tf_op jit(solution)/shard_map/ppermute | solution.py:19
  12.0 1.3 collective-permute-start.1
  15.5 46.0 %all-gather.2.cloned.1.call-done = bf16[16,512,128]{2,1,0:T(8,128)(2,1)} async-done(((bf16[2,512,128]{2,1,0:T(8,128)(2,1)}), bf16[16,512,128]{2,1,0:T(8,128)(2,1)}) %all-gather.2.cloned.1.call-update) | async-done | bytes 2097168 | tf_op jit(solution)/shard_map/all_gather | solution.py:70
  61.5 14.9 %while.38 = (s32[]{:T(128)}, f32[2,8,1,384]{3,2,1,0:T(1,128)}, bf16[2,8,512,128]{3,2,1,0:T(8,128)(2,1)}, bf16[1,256,512]{2,1,0:T(8,128)(2,1)S(1)}, s32[]{:T(128)}) while((s32[]{:T(128)}, f32[2,8,1,384]{3,2,1,0:T(1,128)}, bf16[2,8,512,128]{3,2,1,0:T(8,128)(2,1)}, bf16[1,256,512]{2,1,0:T(8,128)(2,1)S(1)}, s32[]{:T(128)}) %tuple.126), condition=%wide.region_2.3_spmd, body=%wide.region_0.2_spmd.sunk | while | flops 281021440 | bytes 108389440 | solution.py:91
  61.5 1.7 convolution_bitcast_fusion.3
  69.0 1.7 convolution_bitcast_fusion.3
  76.4 3.3 %all-to-all-start = ((f32[8,2,1,384]{3,2,1,0:T(1,128)}), f32[8,2,1,384]{3,2,1,0:T(1,128)S(1)}, u32[]{:S(2)}, u32[]{:S(2)}) async-start(f32[8,2,1,384]{3,2,1,0:T(1,128)} %bitcast.12), calls=%async_computation | async-start | bytes 49152 | tf_op jit(solution)/shard_map/all_to_all | solution.py:93
  79.9 6.4 %all-to-all-done = f32[8,2,1,384]{3,2,1,0:T(1,128)S(1)} async-done(((f32[8,2,1,384]{3,2,1,0:T(1,128)}), f32[8,2,1,384]{3,2,1,0:T(1,128)S(1)}, u32[]{:S(2)}, u32[]{:S(2)}) %all-to-all-start) | async-done | bytes 24608 | tf_op jit(solution)/shard_map/all_to_all | solution.py:93
  86.3 35.3 %while.39 = (s32[]{:T(128)}, f32[1,2,2816]{2,1,0:T(2,128)S(1)}, s32[2,8]{1,0:T(2,128)S(1)}, f32[8,2,1,384]{3,2,1,0:T(1,128)S(1)}, s32[]{:T(128)}, /*index=5*/s32[]{:T(128)}, s32[]{:T(128)}, s32[]{}) while((s32[]{:T(128)}, f32[1,2,2816]{2,1,0:T(2,128)S(1)}, s32[2,8]{1,0:T(2,128)S(1)}, f32[8,2,1,384]{3,2,1,0:T(1,128)S(1)}, s32[]{:T(128)}, ...), condition=%wide.region_4.5_spmd, body=%wide.region_3.4_spmd.sunk | while | flops 777 | bytes 15573 | solution.py:100
  121.7 10.3 %psum.7 = f32[1,2,2816]{2,1,0:T(2,128)S(1)} all-reduce(f32[1,2,2816]{2,1,0:T(2,128)S(1)} %get-tuple-element.160), channel_id=1, replica_groups=mesh['blk'=8,'gy'=4] {'gy'}, use_global_device_ids=true, to_apply=%region_5.6 | all-reduce | flops 5632 | bytes 45056 | tf_op jit(solution)/shard_map/psum | solution.py:101
  132.0 11.8 %while.40 = (s32[]{:T(128)}, bf16[1,2816]{1,0:T(2,128)(2,1)S(1)}, s32[8,2]{0,1:T(2,128)S(1)}, bf16[8,1,384]{2,0,1:T(8,128)(2,1)S(1)}, s32[]{:T(128)}, /*index=5*/s32[]{:T(128)}) while((s32[]{:T(128)}, bf16[1,2816]{1,0:T(2,128)(2,1)S(1)}, s32[8,2]{0,1:T(2,128)S(1)}, bf16[8,1,384]{2,0,1:T(8,128)(2,1)S(1)}, s32[]{:T(128)}, /*index=5*/s32[]{:T(128)}) %tuple.118), condition=%wide.while_cond, body=%wide.while_body.sunk | while | flops 2 | bytes 3177 | solution.py:106
  143.9 10.7 %while.41 = (s32[]{:T(128)}, bf16[1,2816]{1,0:T(2,128)(2,1)S(1)}, s32[8,2]{0,1:T(2,128)S(1)}, bf16[8,1,384]{2,0,1:T(8,128)(2,1)S(1)}, s32[]{:T(128)}, /*index=5*/s32[]{:T(128)}) while((s32[]{:T(128)}, bf16[1,2816]{1,0:T(2,128)(2,1)S(1)}, s32[8,2]{0,1:T(2,128)S(1)}, bf16[8,1,384]{2,0,1:T(8,128)(2,1)S(1)}, s32[]{:T(128)}, /*index=5*/s32[]{:T(128)}) %tuple.115), condition=%wide.while_cond.1, body=%wide.while_body.1.sunk | while | flops 2 | bytes 3177 | solution.py:106
  155.2 3.5 %all-to-all-start.1 = ((bf16[1,8,2,384]{3,2,0,1:T(2,128)(2,1)}), bf16[1,8,2,384]{3,2,0,1:T(2,128)(2,1)S(1)}, u32[]{:S(2)}, u32[]{:S(2)}) async-start(bf16[1,8,2,384]{3,2,0,1:T(2,128)(2,1)} %copy.33), calls=%async_computation.1 | async-start | bytes 24576 | tf_op jit(solution)/shard_map/all_to_all | solution.py:116
  158.7 1.9 maximum_convert_fusion
  160.6 4.4 %all-to-all-done.1 = bf16[1,8,2,384]{3,2,0,1:T(2,128)(2,1)S(1)} async-done(((bf16[1,8,2,384]{3,2,0,1:T(2,128)(2,1)}), bf16[1,8,2,384]{3,2,0,1:T(2,128)(2,1)S(1)}, u32[]{:S(2)}, u32[]{:S(2)}) %all-to-all-start.1) | async-done | bytes 12320 | tf_op jit(solution)/shard_map/all_to_all | solution.py:116
  165.0 29.1 %while.42 = (s32[]{:T(128)}, f32[1,256,512]{2,1,0:T(8,128)}, bf16[2,1,8,384]{3,2,0,1:T(8,128)(2,1)S(1)}, bf16[2,8,512,128]{3,2,1,0:T(8,128)(2,1)}, s32[]{:T(128)}, /*index=5*/s32[]{:T(128)}) while((s32[]{:T(128)}, f32[1,256,512]{2,1,0:T(8,128)}, bf16[2,1,8,384]{3,2,0,1:T(8,128)(2,1)S(1)}, bf16[2,8,512,128]{3,2,1,0:T(8,128)(2,1)}, ...), condition=%wide.region_7.8_spmd.clone, body=%wide.region_6.7_spmd.clone.sunk | while | flops 301471744 | bytes 67193432 | solution.py:131
  167.1 1.1 maximum_select_fusion.34
  176.3 0.9 slice.383
  177.2 2.3 %fusion.41 = f32[1,256,512]{2,1,0:T(8,128)} fusion(bf16[2,8,512,128]{3,2,1,0:T(8,128)(2,1)S(1)} %copy-done, s32[]{:T(128)} %get-tuple-element.503, bf16[1,8,256,128]{3,2,1,0:T(8,128)(2,1)} %slice.383, bf16[1,8,256,256]{3,2,1,0:T(8,128)(2,1)S(1)} %slice.384, f32[1,256,512]{2,1,0:T(8,128)} %get-tuple-element.504, ...), kind=kOutput, calls=%fused_computation.42.clone.1 | convolution fusion | flops 270008320 | bytes 3670533 | tf_op jit(solution)/shard_map/while/body/eval_jaxpr/ytid,tzd->yiz/dot_general | solution.py:125
  181.6 1.1 maximum_select_fusion.34
  190.8 0.9 slice.383
  191.7 2.5 %fusion.41 = f32[1,256,512]{2,1,0:T(8,128)} fusion(bf16[2,8,512,128]{3,2,1,0:T(8,128)(2,1)S(1)} %copy-done, s32[]{:T(128)} %get-tuple-element.503, bf16[1,8,256,128]{3,2,1,0:T(8,128)(2,1)} %slice.383, bf16[1,8,256,256]{3,2,1,0:T(8,128)(2,1)S(1)} %slice.384, f32[1,256,512]{2,1,0:T(8,128)} %get-tuple-element.504, ...), kind=kOutput, calls=%fused_computation.42.clone.1 | convolution fusion | flops 270008320 | bytes 3670533 | tf_op jit(solution)/shard_map/while/body/eval_jaxpr/ytid,tzd->yiz/dot_general | solution.py:125
  194.2 2.8 %fusion.19 = f32[1,256,512]{2,1,0:T(8,128)} fusion(f32[1,256,514]{2,1,0:T(8,128)} %maximum_convert_fusion, f32[1,256,512]{2,1,0:T(8,128)} %param.12, f32[1,256,512]{2,1,0:T(8,128)} %get-tuple-element.161, f32[256,512]{1,0:T(8,128)} %param.15), kind=kLoop, calls=%fused_computation.65 | loop fusion | flops 917504 | bytes 3145728 | tf_op jit(solution)/shard_map/add | solution.py:134
  (271 shorter events, 65.8 us)
Async XLA Ops:
  6.5 55.0 %all-gather.2.cloned.1.call-start = ((), (), s32[]{:S(2)}) async-start(), calls=%async_computation.2 | async-start | bytes 2359296 | tf_op jit(solution)/shard_map/all_gather | solution.py:70
  9.0 149.7 %collective-permute-start = (bf16[1,256,1]{2,1,0:T(8,128)(2,1)}, bf16[1,256,1]{2,1,0:T(8,128)(2,1)}, u32[]{:S(2)}, u32[]{:S(2)}) collective-permute-start(bf16[1,256,1]{2,1,0:T(8,128)(2,1)} %get-tuple-element.283), channel_id=1, source_target_pairs={{0,1},{1,2},{2,3},{4,5},{5,6},{6,7},{8,9},{9,10},{10,11},{12,13},{... | collective-permute-start | bytes 1544 | tf_op jit(solution)/shard_map/ppermute | solution.py:19
  12.0 146.7 %collective-permute-start.1 = (bf16[1,256,1]{2,1,0:T(8,128)(2,1)}, bf16[1,256,1]{2,1,0:T(8,128)(2,1)}, u32[]{:S(2)}, u32[]{:S(2)}) collective-permute-start(bf16[1,256,1]{2,1,0:T(8,128)(2,1)} %get-tuple-element.284), channel_id=1, source_target_pairs={{1,0},{2,1},{3,2},{5,4},{6,5},{7,6},{9,8},{10,9},{11,10},{13,12},{... | collective-permute-start | bytes 1544 | tf_op jit(solution)/shard_map/ppermute | solution.py:21
  14.2 0.6 copy-start.1
  61.5 18.3 %copy-start.5 = (s32[8]{0:T(128)S(1)}, s32[8]{0:T(128)}, u32[]{:S(2)}) copy-start(s32[8]{0:T(128)} %get-tuple-element.237) | copy-start | bytes 100
  61.5 18.3 %copy-start.6 = (s32[8]{0:T(128)S(1)}, s32[8]{0:T(128)}, u32[]{:S(2)}) copy-start(s32[8]{0:T(128)} %get-tuple-element.238) | copy-start | bytes 100
  61.5 18.3 %copy-start.2 = (s32[2,8]{0,1:T(8,128)S(1)}, s32[2,8]{0,1:T(8,128)}, u32[]{:S(2)}) copy-start(s32[2,8]{0,1:T(8,128)} %copy-done.1) | copy-start | bytes 196
  61.5 70.4 %copy-start.3 = (f32[2,2816]{1,0:T(2,128)S(1)}, f32[2,2816]{1,0:T(2,128)}, u32[]{:S(2)}) copy-start(f32[2,2816]{1,0:T(2,128)} %param.14) | copy-start | bytes 67588
  61.5 70.4 %copy-start.4 = (f32[1,2,2816]{2,1,0:T(2,128)S(1)}, f32[1,2,2816]{2,1,0:T(2,128)}, u32[]{:S(2)}) copy-start(f32[1,2,2816]{2,1,0:T(2,128)} %param.13) | copy-start | bytes 67588
  76.4 9.9 %all-to-all-start = ((f32[8,2,1,384]{3,2,1,0:T(1,128)}), f32[8,2,1,384]{3,2,1,0:T(1,128)S(1)}, u32[]{:S(2)}, u32[]{:S(2)}) async-start(f32[8,2,1,384]{3,2,1,0:T(1,128)} %bitcast.12), calls=%async_computation | async-start | bytes 49152 | tf_op jit(solution)/shard_map/all_to_all | solution.py:93
  155.2 9.8 %all-to-all-start.1 = ((bf16[1,8,2,384]{3,2,0,1:T(2,128)(2,1)}), bf16[1,8,2,384]{3,2,0,1:T(2,128)(2,1)S(1)}, u32[]{:S(2)}, u32[]{:S(2)}) async-start(bf16[1,8,2,384]{3,2,0,1:T(2,128)(2,1)} %copy.33), calls=%async_computation.1 | async-start | bytes 24576 | tf_op jit(solution)/shard_map/all_to_all | solution.py:116
  175.5 1.7 copy-start
  190.0 1.7 copy-start
Sparse Core Ops, SparseCore 0:
  9.5 51.9 all-gather.1
where the time goes:
time: 205 us; the launch traced here: 204 us
  waiting for transfers between devices  57.6 us (28%)
  local copies, waits for them, and re-layouts  49.3 us (24%)
  loops' own time  28.2 us (14%)
  other arithmetic  25.6 us (12%)
  between operations  13.6 us (7%)
  starting transfers between devices  11.1 us (5%)
  blocking collectives  10.3 us (5%)
  matrix products  8.25 us (4%)
    all_gather x1, waiting for transfers between devices, per_device(): all_weights = lax.all_gather(band_weight, 'blk', axis=0, tiled=True)  46 us
    another operation x1, loops' own time, per_device(): partial_sum = lax.fori_loop(0, block_count, add_source, initial)  27.2 us
    gather x64, local copies, waits for them, and re-layouts  22.3 us
    select_n x28, other arithmetic, shift_rows(): rows = jnp.where(chosen, moved, rows)  16.4 us
    slice x60, local copies, waits for them, and re-layouts, shift_rows(): moved = jnp.roll(rows, direction * (1 << level), axis=-1)  15.1 us
    psum x1, blocking collectives, per_device(): projection = lax.psum(partial_sum, 'gy')  10.3 us
    all_to_all x1, waiting for transfers between devices, per_device(): lax.all_to_all(windows, 'blk', split_axis=0, concat_axis=0, tiled=True)  6.42 us
    dot_general x2, matrix products, back_group(): jnp.einsum('ytid,tzd->yiz', sheared, weight_part, preferred_element_type=...  4.81 us
  transfers between devices with their start and end apart: 5, of which 3 were waited for; matrix products, arithmetic and copies ran while one was open for 25% of the time, Pallas kernels for 0%

commit v1 on v0

--- a/solution.py
+++ b/solution.py
@@ -6,6 +6,13 @@
 
 PW = 128
 SMOOTH = 0.25
+
+
+def stacked_exchange(x, axis, split, join):
+    n_dev = lax.axis_size(axis)
+    blocks = jnp.stack(jnp.split(x, n_dev, axis=split), axis=0)
+    blocks = lax.all_to_all(blocks, axis, split_axis=0, concat_axis=0)
+    return jnp.concatenate(blocks, axis=join)
 
 
 def with_halo(cells, sides, width):
@@ -113,7 +120,7 @@
         return jnp.stack(pieces, axis=1)
 
     outgoing = jax.vmap(cut_panels, in_axes=1, out_axes=1)(own_bins)
-    arrived = lax.all_to_all(outgoing, "blk", split_axis=1, concat_axis=1, tiled=True)
+    arrived = stacked_exchange(outgoing, "blk", 1, 1)
     panels = arrived.reshape(row_count, tilt_count, window_len)
     panel_groups = panels.reshape(
         row_count, tilt_count // group_size, group_size, window_len

time: 205 us -> 211 us (1.029)
  local copies, waits for them, and re-layouts: 49.3 us -> 53.3 us
  loops' own time: 28.2 us -> 30.5 us
    unnamed x14 -> x21, local copies, waits for them, and re-layouts: 0.62 us -> 4.58 us
    another operation x1, loops' own time: 27.2 us -> 29.5 us  [per_device(): partial_sum = lax.fori_loop(0, block_count, add_source, initial)]
  transfers between devices with their start and end apart: 5 -> 5, of which waited for: 3 -> 3; matrix products, arithmetic and copies ran while one was open for 25% -> 26% of each run, Pallas kernels for 0% -> 0%
where the time goes in v1:
time: 211 us; the launch traced here: 210 us
  waiting for transfers between devices  57.5 us (27%)
  local copies, waits for them, and re-layouts  53.3 us (25%)
  loops' own time  30.5 us (14%)
  other arithmetic  25.6 us (12%)
  between operations  13.6 us (6%)
  starting transfers between devices  11.1 us (5%)
  blocking collectives  10.3 us (5%)
  matrix products  8.26 us (4%)
    all_gather x1, waiting for transfers between devices, per_device(): all_weights = lax.all_gather(band_weight, 'blk', axis=0, tiled=True)  46 us
    another operation x1, loops' own time, per_device(): partial_sum = lax.fori_loop(0, block_count, add_source, initial)  29.5 us
    gather x64, local copies, waits for them, and re-layouts  21.9 us
    select_n x28, other arithmetic, shift_rows(): rows = jnp.where(chosen, moved, rows)  16.4 us
    slice x60, local copies, waits for them, and re-layouts, shift_rows(): moved = jnp.roll(rows, direction * (1 << level), axis=-1)  15.1 us
    psum x1, blocking collectives, per_device(): projection = lax.psum(partial_sum, 'gy')  10.3 us
    all_to_all x1, waiting for transfers between devices, per_device(): lax.all_to_all(windows, 'blk', split_axis=0, concat_axis=0, tiled=True)  6.42 us
    dynamic_slice x8, local copies, waits for them, and re-layouts, place_windows(): offset = own_bins[tilt_slot, source]  5.2 us
  transfers between devices with their start and end apart: 5, of which 3 were waited for; matrix products, arithmetic and copies ran while one was open for 26% of the time, Pallas kernels for 0%

profile of v1, /device:TPU:0, one launch (start us, length us, event | category | flops | bytes accessed | tf_op | source)
XLA Modules:
  0.0 210.1 jit_solution(7843924293539976151)
XLA Ops:
  7.3 1.1 convert_element_type.22
  9.0 3.0 %collective-permute-start = (bf16[1,256,1]{2,1,0:T(8,128)(2,1)}, bf16[1,256,1]{2,1,0:T(8,128)(2,1)}, u32[]{:S(2)}, u32[]{:S(2)}) collective-permute-start(bf16[1,256,1]{2,1,0:T(8,128)(2,1)} %get-tuple-element.339), channel_id=1, source_target_pairs={{0,1},{1,2},{2,3},{4,5},{5,6},{6,7},{8,9},{9,10},{10,11},{12,13},{... | collective-permute-start | bytes 1544 | tf_op jit(solution)/shard_map/ppermute | solution.py:26
  12.0 1.3 collective-permute-start.1
  15.5 46.0 %all-gather.2.cloned.1.call-done = bf16[16,512,128]{2,1,0:T(8,128)(2,1)} async-done(((bf16[2,512,128]{2,1,0:T(8,128)(2,1)}), bf16[16,512,128]{2,1,0:T(8,128)(2,1)}) %all-gather.2.cloned.1.call-update) | async-done | bytes 2097168 | tf_op jit(solution)/shard_map/all_gather | solution.py:77
  61.5 14.9 %while.38 = (s32[]{:T(128)}, f32[2,8,1,384]{3,2,1,0:T(1,128)}, bf16[2,8,512,128]{3,2,1,0:T(8,128)(2,1)}, bf16[1,256,512]{2,1,0:T(8,128)(2,1)S(1)}, s32[]{:T(128)}) while((s32[]{:T(128)}, f32[2,8,1,384]{3,2,1,0:T(1,128)}, bf16[2,8,512,128]{3,2,1,0:T(8,128)(2,1)}, bf16[1,256,512]{2,1,0:T(8,128)(2,1)S(1)}, s32[]{:T(128)}) %tuple.147), condition=%wide.region_2.3_spmd, body=%wide.region_0.2_spmd.sunk | while | flops 281021440 | bytes 108389440 | solution.py:98
  61.5 1.7 convolution_bitcast_fusion.3
  69.0 1.7 convolution_bitcast_fusion.3
  76.4 3.3 %all-to-all-start = ((f32[8,2,1,384]{3,2,1,0:T(1,128)}), f32[8,2,1,384]{3,2,1,0:T(1,128)S(1)}, u32[]{:S(2)}, u32[]{:S(2)}) async-start(f32[8,2,1,384]{3,2,1,0:T(1,128)} %bitcast.12), calls=%async_computation | async-start | bytes 49152 | tf_op jit(solution)/shard_map/all_to_all | solution.py:100
  79.9 6.4 %all-to-all-done = f32[8,2,1,384]{3,2,1,0:T(1,128)S(1)} async-done(((f32[8,2,1,384]{3,2,1,0:T(1,128)}), f32[8,2,1,384]{3,2,1,0:T(1,128)S(1)}, u32[]{:S(2)}, u32[]{:S(2)}) %all-to-all-start) | async-done | bytes 24608 | tf_op jit(solution)/shard_map/all_to_all | solution.py:100
  86.3 38.1 %while.39 = (s32[]{:T(128)}, f32[1,2,2816]{2,1,0:T(2,128)S(1)}, s32[2,8]{1,0:T(2,128)S(1)}, f32[8,2,1,384]{3,2,1,0:T(1,128)S(1)}, s32[]{:T(128)}, /*index=5*/s32[]{:T(128)}, s32[]{:T(128)}, s32[]{}) while((s32[]{:T(128)}, f32[1,2,2816]{2,1,0:T(2,128)S(1)}, s32[2,8]{1,0:T(2,128)S(1)}, f32[8,2,1,384]{3,2,1,0:T(1,128)S(1)}, s32[]{:T(128)}, ...), condition=%wide.region_4.5_spmd, body=%wide.region_3.4_spmd.sunk | while | flops 777 | bytes 15573 | solution.py:107
  124.5 10.3 %psum.7 = f32[1,2,2816]{2,1,0:T(2,128)S(1)} all-reduce(f32[1,2,2816]{2,1,0:T(2,128)S(1)} %get-tuple-element.160), channel_id=1, replica_groups=mesh['blk'=8,'gy'=4] {'gy'}, use_global_device_ids=true, to_apply=%region_5.6 | all-reduce | flops 5632 | bytes 45056 | tf_op jit(solution)/shard_map/psum | solution.py:108
  134.8 10.3 %while.40 = (s32[]{:T(128)}, bf16[1,2816]{1,0:T(2,128)(2,1)S(1)}, s32[8,2]{0,1:T(2,128)S(1)}, bf16[8,1,384]{2,0,1:T(8,128)(2,1)S(1)}, s32[]{:T(128)}, /*index=5*/s32[]{:T(128)}) while((s32[]{:T(128)}, bf16[1,2816]{1,0:T(2,128)(2,1)S(1)}, s32[8,2]{0,1:T(2,128)S(1)}, bf16[8,1,384]{2,0,1:T(8,128)(2,1)S(1)}, s32[]{:T(128)}, /*index=5*/s32[]{:T(128)}) %tuple.139), condition=%wide.while_cond, body=%wide.while_body.sunk | while | flops 2 | bytes 3177 | solution.py:113
  145.1 11.8 %while.41 = (s32[]{:T(128)}, bf16[1,2816]{1,0:T(2,128)(2,1)S(1)}, s32[8,2]{0,1:T(2,128)S(1)}, bf16[8,1,384]{2,0,1:T(8,128)(2,1)S(1)}, s32[]{:T(128)}, /*index=5*/s32[]{:T(128)}) while((s32[]{:T(128)}, bf16[1,2816]{1,0:T(2,128)(2,1)S(1)}, s32[8,2]{0,1:T(2,128)S(1)}, bf16[8,1,384]{2,0,1:T(8,128)(2,1)S(1)}, s32[]{:T(128)}, /*index=5*/s32[]{:T(128)}) %tuple.136), condition=%wide.while_cond.1, body=%wide.while_body.1.sunk | while | flops 2 | bytes 3177 | solution.py:113
  161.5 3.5 %all-to-all-start.1 = ((bf16[8,1,1,2,384]{4,3,2,1,0:T(2,128)(2,1)}), bf16[8,1,1,2,384]{4,3,2,1,0:T(2,128)(2,1)S(1)}, u32[]{:S(2)}, u32[]{:S(2)}) async-start(bf16[8,1,1,2,384]{4,3,2,1,0:T(2,128)(2,1)} %constant_dynamic-update-slice_fusion), calls=%async_computation.1 | async-start | bytes 24576 | tf_op jit(solution)/shard_map/all_to_all | solution.py:14
  165.0 1.9 maximum_convert_fusion
  166.9 4.4 %all-to-all-done.1 = bf16[8,1,1,2,384]{4,3,2,1,0:T(2,128)(2,1)S(1)} async-done(((bf16[8,1,1,2,384]{4,3,2,1,0:T(2,128)(2,1)}), bf16[8,1,1,2,384]{4,3,2,1,0:T(2,128)(2,1)S(1)}, u32[]{:S(2)}, u32[]{:S(2)}) %all-to-all-start.1) | async-done | bytes 12320 | tf_op jit(solution)/shard_map/all_to_all | solution.py:14
  171.3 29.2 %while.42 = (s32[]{:T(128)}, f32[1,256,512]{2,1,0:T(8,128)}, bf16[2,1,8,384]{3,2,0,1:T(8,128)(2,1)S(1)}, bf16[2,8,512,128]{3,2,1,0:T(8,128)(2,1)}, s32[]{:T(128)}, /*index=5*/s32[]{:T(128)}) while((s32[]{:T(128)}, f32[1,256,512]{2,1,0:T(8,128)}, bf16[2,1,8,384]{3,2,0,1:T(8,128)(2,1)S(1)}, bf16[2,8,512,128]{3,2,1,0:T(8,128)(2,1)}, ...), condition=%wide.region_7.8_spmd.clone, body=%wide.region_6.7_spmd.clone.sunk | while | flops 301471744 | bytes 67193432 | solution.py:138
  173.4 1.1 maximum_select_fusion.34
  182.6 0.9 slice.383
  183.5 2.3 %fusion.42 = f32[1,256,512]{2,1,0:T(8,128)} fusion(bf16[2,8,512,128]{3,2,1,0:T(8,128)(2,1)S(1)} %copy-done, s32[]{:T(128)} %get-tuple-element.567, bf16[1,8,256,128]{3,2,1,0:T(8,128)(2,1)} %slice.383, bf16[1,8,256,256]{3,2,1,0:T(8,128)(2,1)S(1)} %slice.384, f32[1,256,512]{2,1,0:T(8,128)} %get-tuple-element.568, ...), kind=kOutput, calls=%fused_computation.42.clone.1 | convolution fusion | flops 270008320 | bytes 3670533 | tf_op jit(solution)/shard_map/while/body/eval_jaxpr/ytid,tzd->yiz/dot_general | solution.py:132
  187.9 1.1 maximum_select_fusion.34
  197.1 0.9 slice.383
  198.0 2.5 %fusion.42 = f32[1,256,512]{2,1,0:T(8,128)} fusion(bf16[2,8,512,128]{3,2,1,0:T(8,128)(2,1)S(1)} %copy-done, s32[]{:T(128)} %get-tuple-element.567, bf16[1,8,256,128]{3,2,1,0:T(8,128)(2,1)} %slice.383, bf16[1,8,256,256]{3,2,1,0:T(8,128)(2,1)S(1)} %slice.384, f32[1,256,512]{2,1,0:T(8,128)} %get-tuple-element.568, ...), kind=kOutput, calls=%fused_computation.42.clone.1 | convolution fusion | flops 270008320 | bytes 3670533 | tf_op jit(solution)/shard_map/while/body/eval_jaxpr/ytid,tzd->yiz/dot_general | solution.py:132
  200.5 2.8 %fusion.19 = f32[1,256,512]{2,1,0:T(8,128)} fusion(f32[1,256,514]{2,1,0:T(8,128)} %maximum_convert_fusion, f32[1,256,512]{2,1,0:T(8,128)} %param.12, f32[1,256,512]{2,1,0:T(8,128)} %get-tuple-element.161, f32[256,512]{1,0:T(8,128)} %param.15), kind=kLoop, calls=%fused_computation.65 | loop fusion | flops 917504 | bytes 3145728 | tf_op jit(solution)/shard_map/add | solution.py:141
  (279 shorter events, 69.7 us)
Async XLA Ops:
  6.5 55.0 %all-gather.2.cloned.1.call-start = ((), (), s32[]{:S(2)}) async-start(), calls=%async_computation.2 | async-start | bytes 2359296 | tf_op jit(solution)/shard_map/all_gather | solution.py:77
  9.0 155.9 %collective-permute-start = (bf16[1,256,1]{2,1,0:T(8,128)(2,1)}, bf16[1,256,1]{2,1,0:T(8,128)(2,1)}, u32[]{:S(2)}, u32[]{:S(2)}) collective-permute-start(bf16[1,256,1]{2,1,0:T(8,128)(2,1)} %get-tuple-element.339), channel_id=1, source_target_pairs={{0,1},{1,2},{2,3},{4,5},{5,6},{6,7},{8,9},{9,10},{10,11},{12,13},{... | collective-permute-start | bytes 1544 | tf_op jit(solution)/shard_map/ppermute | solution.py:26
  12.0 153.0 %collective-permute-start.1 = (bf16[1,256,1]{2,1,0:T(8,128)(2,1)}, bf16[1,256,1]{2,1,0:T(8,128)(2,1)}, u32[]{:S(2)}, u32[]{:S(2)}) collective-permute-start(bf16[1,256,1]{2,1,0:T(8,128)(2,1)} %get-tuple-element.340), channel_id=1, source_target_pairs={{1,0},{2,1},{3,2},{5,4},{6,5},{7,6},{9,8},{10,9},{11,10},{13,12},{... | collective-permute-start | bytes 1544 | tf_op jit(solution)/shard_map/ppermute | solution.py:28
  14.2 0.6 copy-start.1
  61.5 18.3 %copy-start.5 = (s32[8]{0:T(128)S(1)}, s32[8]{0:T(128)}, u32[]{:S(2)}) copy-start(s32[8]{0:T(128)} %get-tuple-element.293) | copy-start | bytes 100
  61.5 18.3 %copy-start.6 = (s32[8]{0:T(128)S(1)}, s32[8]{0:T(128)}, u32[]{:S(2)}) copy-start(s32[8]{0:T(128)} %get-tuple-element.294) | copy-start | bytes 100
  61.5 18.3 %copy-start.2 = (s32[2,8]{0,1:T(8,128)S(1)}, s32[2,8]{0,1:T(8,128)}, u32[]{:S(2)}) copy-start(s32[2,8]{0,1:T(8,128)} %copy-done.1) | copy-start | bytes 196
  61.5 73.2 %copy-start.3 = (f32[2,2816]{1,0:T(2,128)S(1)}, f32[2,2816]{1,0:T(2,128)}, u32[]{:S(2)}) copy-start(f32[2,2816]{1,0:T(2,128)} %param.14) | copy-start | bytes 67588
  61.5 73.2 %copy-start.4 = (f32[1,2,2816]{2,1,0:T(2,128)S(1)}, f32[1,2,2816]{2,1,0:T(2,128)}, u32[]{:S(2)}) copy-start(f32[1,2,2816]{2,1,0:T(2,128)} %param.13) | copy-start | bytes 67588
  76.4 9.9 %all-to-all-start = ((f32[8,2,1,384]{3,2,1,0:T(1,128)}), f32[8,2,1,384]{3,2,1,0:T(1,128)S(1)}, u32[]{:S(2)}, u32[]{:S(2)}) async-start(f32[8,2,1,384]{3,2,1,0:T(1,128)} %bitcast.12), calls=%async_computation | async-start | bytes 49152 | tf_op jit(solution)/shard_map/all_to_all | solution.py:100
  161.5 9.8 %all-to-all-start.1 = ((bf16[8,1,1,2,384]{4,3,2,1,0:T(2,128)(2,1)}), bf16[8,1,1,2,384]{4,3,2,1,0:T(2,128)(2,1)S(1)}, u32[]{:S(2)}, u32[]{:S(2)}) async-start(bf16[8,1,1,2,384]{4,3,2,1,0:T(2,128)(2,1)} %constant_dynamic-update-slice_fusion), calls=%async_computation.1 | async-start | bytes 24576 | tf_op jit(solution)/shard_map/all_to_all | solution.py:14
  181.7 1.7 copy-start
  196.3 1.7 copy-start
Sparse Core Ops, SparseCore 0:
  9.5 51.9 all-gather.1
